TPU v7x, 32 devices: a whole 2x2x4 slice. The times are simulated.
32 devices in a mesh: dp: 4 (over x, core), fsdp: 8 (over z, y).
Axes of the slice: x: 2, y: 2, z: 4, core: 2. Of those that a mesh axis runs over, the one named last changes fastest.
Arguments:
- frames: bfloat16 [32, 512, 512], P(('dp', 'fsdp')), may hold values from -12 to 12
- cotangent: bfloat16 [32, 512, 512], P(('dp', 'fsdp')), may hold values from -6 to 6
- seq_lengths: int32 [32], P(('dp', 'fsdp')), may hold values from 64 to 512, as said below
- ffn_in_master: float32 [2, 512, 2048], P(None, ('dp', 'fsdp')), may hold values from -0.25 to 0.25
- ffn_out_master: float32 [2, 2048, 512], P(None, ('dp', 'fsdp')), may hold values from -0.125 to 0.125
- mix_in_master: float32 [2, 512, 1024], P(None, ('dp', 'fsdp')), may hold values from -0.25 to 0.25
- mix_out_master: float32 [2, 512, 512], P(None, ('dp', 'fsdp')), may hold values from -0.25 to 0.25
- vector_master: float32 [30, 512], P(None, ('dp', 'fsdp')), may hold values from -5.3 to 2
- ffn_in_first: float32 [2, 512, 2048], P(None, ('dp', 'fsdp')), may hold values from -112 to 112
- ffn_out_first: float32 [2, 2048, 512], P(None, ('dp', 'fsdp')), may hold values from -160 to 160
- mix_in_first: float32 [2, 512, 1024], P(None, ('dp', 'fsdp')), may hold values from -160 to 160
- mix_out_first: float32 [2, 512, 512], P(None, ('dp', 'fsdp')), may hold values from -320 to 320
- vector_first: float32 [30, 512], P(None, ('dp', 'fsdp')), may hold values from -384 to 384
- ffn_in_second: float32 [2, 512, 2048], P(None, ('dp', 'fsdp')), may hold values from 184.32 to 1474.56
- ffn_out_second: float32 [2, 2048, 512], P(None, ('dp', 'fsdp')), may hold values from 327.68 to 2621.44
- mix_in_second: float32 [2, 512, 1024], P(None, ('dp', 'fsdp')), may hold values from 327.68 to 2621.44
- mix_out_second: float32 [2, 512, 512], P(None, ('dp', 'fsdp')), may hold values from 1310.72 to 10485.76
- vector_second: float32 [30, 512], P(None, ('dp', 'fsdp')), may hold values from 2048 to 16384
Outputs:
- activations: float32 [32, 512, 512], P(('dp', 'fsdp'))
- input_grad: float32 [32, 512, 512], P(('dp', 'fsdp'))
- ffn_in_new: float32 [2, 512, 2048], P(None, ('dp', 'fsdp'))
- ffn_out_new: float32 [2, 2048, 512], P(None, ('dp', 'fsdp'))
- mix_in_new: float32 [2, 512, 1024], P(None, ('dp', 'fsdp'))
- mix_out_new: float32 [2, 512, 512], P(None, ('dp', 'fsdp'))
- vector_new: float32 [30, 512], P(None, ('dp', 'fsdp'))
- ffn_in_first_new: float32 [2, 512, 2048], P(None, ('dp', 'fsdp'))
- ffn_out_first_new: float32 [2, 2048, 512], P(None, ('dp', 'fsdp'))
- mix_in_first_new: float32 [2, 512, 1024], P(None, ('dp', 'fsdp'))
- mix_out_first_new: float32 [2, 512, 512], P(None, ('dp', 'fsdp'))
- vector_first_new: float32 [30, 512], P(None, ('dp', 'fsdp'))
- ffn_in_second_new: float32 [2, 512, 2048], P(None, ('dp', 'fsdp'))
- ffn_out_second_new: float32 [2, 2048, 512], P(None, ('dp', 'fsdp'))
- mix_in_second_new: float32 [2, 512, 1024], P(None, ('dp', 'fsdp'))
- mix_out_second_new: float32 [2, 512, 512], P(None, ('dp', 'fsdp'))
- vector_second_new: float32 [30, 512], P(None, ('dp', 'fsdp'))
- ffn_in_copy: bfloat16 [2, 512, 2048], P(None, ('dp', 'fsdp'))
- ffn_out_copy: bfloat16 [2, 2048, 512], P(None, ('dp', 'fsdp'))
- mix_in_copy: bfloat16 [2, 512, 1024], P(None, ('dp', 'fsdp'))
- mix_out_copy: bfloat16 [2, 512, 512], P(None, ('dp', 'fsdp'))
- vector_copy: bfloat16 [30, 512], P(None, ('dp', 'fsdp'))
- sublayer_rms: float32 [5], replicated
Inputs may be any that keep to these rules, and one draw needn't show every extreme that they name: `seq_lengths`: every draw holds a sequence of length 512 and one of length 64.
All inputs are finite; a program needn't handle non-finite values.
Results may differ from a plain program's by a relative error of at most 0.022.
The roundings to bfloat16 on the way count: a program that leaves them out, or rounds other values in their place, can miss the bound.
Values may be sent and summed in bfloat16 or wider, within the bound.
No kernel may reach another device: no remote copies, remote signals or barrier semaphores. Data moves between devices by JAX's collectives and lax.ppermute only.
A program may use at most 192 MiB of HBM per device.

v0:
```python
import jax
import jax.numpy as jnp
from jax import lax
from jax.sharding import PartitionSpec as P

HEADS = 8
NSTATE = 32
KERNEL = 15
STEP_NUMBER = 5


NORM_EPS = 1e-05
BETA_FIRST = 0.5
BETA_SECOND = 0.6
ADAM_EPS = 1e-08
RATE_MATRIX = 0.02
RATE_VECTOR = 0.2
WEIGHT_DECAY = 0.01
HIGHEST = lax.Precision.HIGHEST
skip_row = 12
ssm_row = 13
tap_first = 14


def layer_norm(values, vectors, norm_index):
    scale_row = vectors[2 * norm_index]
    shift_row = vectors[2 * norm_index + 1]
    average = jnp.mean(values, axis=-1, keepdims=True)
    centered = values - average
    variance = jnp.mean(centered * centered, axis=-1, keepdims=True)
    return centered * lax.rsqrt(variance + NORM_EPS) * scale_row + shift_row


def causal_toeplitz(kernel):
    head_count, length = kernel.shape
    backward_row = jnp.concatenate(
        [jnp.flip(kernel, axis=1), jnp.zeros((head_count, length), jnp.float32)], axis=1
    )
    repeated = jnp.broadcast_to(backward_row[:, None, :], (head_count, length, 2 * length)).reshape(
        head_count, 2 * length * length
    )
    skewed = repeated[:, : length * (2 * length - 1)].reshape(head_count, length, 2 * length - 1)
    return skewed[:, :, length - 1 :]


def long_conv(signal, vectors):
    seq_count, length, channels = signal.shape
    states = NSTATE
    decay_logs = vectors[ssm_row, : HEADS * states].reshape(HEADS, states)
    coefficient = vectors[ssm_row, HEADS * states :].reshape(HEADS, states)
    decay_rates = jnp.exp(decay_logs)
    lag_times = jnp.arange(length).astype(jnp.float32)
    kernel = jnp.sum(
        coefficient[:, :, None] * jnp.exp(-decay_rates[:, :, None] * lag_times[None, None, :]),
        axis=1,
    )
    toeplitz = causal_toeplitz(kernel)
    by_head = signal.reshape(seq_count, length, HEADS, channels // HEADS)
    convolved = jnp.einsum("hts,bshc->bthc", toeplitz, by_head, precision=HIGHEST)
    return convolved.reshape(seq_count, length, channels) + vectors[skip_row] * signal


def ssm_piece(projected, valid, vectors):
    channels = projected.shape[-1] // 2
    signal = projected[..., :channels] * valid
    gate_part = projected[..., channels:]
    return long_conv(signal, vectors) * jax.nn.silu(gate_part)


def conv_piece(projected, valid, vectors):
    channels = projected.shape[-1] // 2
    length = projected.shape[1]
    glu_out = projected[..., :channels] * jax.nn.sigmoid(projected[..., channels:]) * valid
    margin = KERNEL // 2
    padded = jnp.pad(glu_out, ((0, 0), (margin, margin), (0, 0)))
    summed = vectors[tap_first + KERNEL] + padded[:, 0:length] * vectors[tap_first]
    for offset in range(1, KERNEL):
        summed = summed + padded[:, offset : offset + length] * vectors[tap_first + offset]
    return jax.nn.silu(layer_norm(summed, vectors, 3))


def adamw(master, first, second, gradient, rate, decay):
    first_new = BETA_FIRST * first + (1.0 - BETA_FIRST) * gradient
    second_new = BETA_SECOND * second + (1.0 - BETA_SECOND) * gradient * gradient
    first_hat = first_new / (1.0 - BETA_FIRST**STEP_NUMBER)
    second_hat = second_new / (1.0 - BETA_SECOND**STEP_NUMBER)
    updated = master - rate * (first_hat / (jnp.sqrt(second_hat) + ADAM_EPS) + decay * master)
    return (updated, first_new, second_new, updated.astype(jnp.bfloat16))


def matmul(left_side, right_side):
    return jnp.dot(left_side, right_side, preferred_element_type=jnp.float32)


def inner_rows(left_side, right_side):
    return lax.dot_general(
        left_side, right_side, (((0,), (0,)), ((), ())), preferred_element_type=jnp.float32
    )


def inner_cols(left_side, right_side):
    return lax.dot_general(
        left_side, right_side, (((1,), (1,)), ((), ())), preferred_element_type=jnp.float32
    )


def run_branch(residual, norm_index, weight_in, weight_out, local_fn, vectors):
    seq_count, length, channels = residual.shape
    normed, pull_norm = jax.vjp(
        lambda values, params: layer_norm(values, params, norm_index), residual, vectors
    )
    normed_low = normed.astype(jnp.bfloat16).reshape(seq_count * length, channels)
    projected = matmul(normed_low, weight_in).reshape(seq_count, length, -1)
    activated, pull_local = jax.vjp(local_fn, projected, vectors)
    active_low = activated.astype(jnp.bfloat16).reshape(seq_count * length, -1)
    output = matmul(active_low, weight_out).reshape(seq_count, length, channels)
    return (output, (pull_norm, normed_low, pull_local, active_low))


def back_branch(grad_output, saved, weight_in, weight_out):
    pull_norm, normed_low, pull_local, active_low = saved
    seq_count, length, channels = grad_output.shape
    grad_low = grad_output.reshape(seq_count * length, channels).astype(jnp.bfloat16)
    grad_out_weight = inner_rows(active_low, grad_low)
    grad_active = inner_cols(grad_low, weight_out).reshape(seq_count, length, -1)
    grad_projected, grad_vec_local = pull_local(grad_active)
    grad_proj_low = grad_projected.reshape(seq_count * length, -1).astype(jnp.bfloat16)
    grad_in_weight = inner_rows(normed_low, grad_proj_low)
    grad_normed = inner_cols(grad_proj_low, weight_in).reshape(seq_count, length, channels)
    grad_residual, grad_vec_norm = pull_norm(grad_normed)
    return (grad_residual, grad_in_weight, grad_out_weight, grad_vec_local + grad_vec_norm)


def local(
    frames,
    cotangent,
    seq_lengths,
    ffn_in_master,
    ffn_out_master,
    mix_in_master,
    mix_out_master,
    vector_master,
    ffn_in_first,
    ffn_out_first,
    mix_in_first,
    mix_out_first,
    vector_first,
    ffn_in_second,
    ffn_out_second,
    mix_in_second,
    mix_out_second,
    vector_second,
):
    seq_count, length, channels = frames.shape
    ffn_in_low = ffn_in_master.astype(jnp.bfloat16)
    ffn_out_low = ffn_out_master.astype(jnp.bfloat16)
    mix_in_low = mix_in_master.astype(jnp.bfloat16)
    mix_out_low = mix_out_master.astype(jnp.bfloat16)
    vector_low = vector_master.astype(jnp.bfloat16)
    gathered = (
        lax.all_gather(ffn_in_low, ("dp", "fsdp"), axis=1, tiled=True),
        lax.all_gather(ffn_out_low, ("dp", "fsdp"), axis=1, tiled=True),
        lax.all_gather(mix_in_low, ("dp", "fsdp"), axis=1, tiled=True),
        lax.all_gather(mix_out_low, ("dp", "fsdp"), axis=1, tiled=True),
        lax.all_gather(vector_low, ("dp", "fsdp"), axis=1, tiled=True),
    )
    vectors = gathered[4].astype(jnp.float32)
    positions = jnp.arange(length, dtype=jnp.int32)
    valid = (positions[None, :] < seq_lengths[:, None]).astype(jnp.float32)[:, :, None]

    def silu_fn(projected, params):
        return jax.nn.silu(projected)

    def ssm_fn(projected, params):
        return ssm_piece(projected, valid, params)

    def conv_fn(projected, params):
        return conv_piece(projected, valid, params)

    local_fns = (silu_fn, ssm_fn, conv_fn, silu_fn)
    norm_indices = (0, 1, 2, 4)
    scales = (0.5, 1.0, 1.0, 0.5)
    stack_index = (0, 0, 1, 1)
    is_ffn = (True, False, False, True)

    def weight_pair(weights, module):
        which = stack_index[module]
        if is_ffn[module]:
            return (weights[0][which], weights[1][which])
        return (weights[2][which], weights[3][which])

    residual = frames.astype(jnp.float32)
    saved_all = []
    piece_outs = []
    for module in range(4):
        weight_in, weight_out = weight_pair(gathered, module)
        output, saved = run_branch(
            residual, norm_indices[module], weight_in, weight_out, local_fns[module], vectors
        )
        branch_part = scales[module] * output
        piece_outs.append(branch_part)
        saved_all.append(saved)
        residual = residual + branch_part
    activations, pull_final = jax.vjp(
        lambda values, params: layer_norm(values, params, 5), residual, vectors
    )
    piece_outs.append(residual)
    squares = [jnp.sum(valid * piece_out * piece_out) for piece_out in piece_outs]
    local_stats = jnp.stack(squares + [jnp.sum(valid)])
    global_stats = lax.psum(local_stats, ("dp", "fsdp"))
    grad_residual, grad_vectors = pull_final(cotangent.astype(jnp.float32))
    back_weights = (
        lax.all_gather(ffn_in_low, ("dp", "fsdp"), axis=1, tiled=True),
        lax.all_gather(ffn_out_low, ("dp", "fsdp"), axis=1, tiled=True),
        lax.all_gather(mix_in_low, ("dp", "fsdp"), axis=1, tiled=True),
        lax.all_gather(mix_out_low, ("dp", "fsdp"), axis=1, tiled=True),
        lax.all_gather(vector_low, ("dp", "fsdp"), axis=1, tiled=True),
    )
    grad_ins = [None, None, None, None]
    grad_outs = [None, None, None, None]
    for module in (3, 2, 1, 0):
        weight_in, weight_out = weight_pair(back_weights, module)
        grad_branch, grad_in_weight, grad_out_weight, grad_vec_more = back_branch(
            scales[module] * grad_residual, saved_all[module], weight_in, weight_out
        )
        grad_residual = grad_residual + grad_branch
        grad_vectors = grad_vectors + grad_vec_more
        grad_ins[module] = grad_in_weight
        grad_outs[module] = grad_out_weight
    grad_ffn_in = jnp.stack([grad_ins[0], grad_ins[3]])
    grad_ffn_out = jnp.stack([grad_outs[0], grad_outs[3]])
    grad_mix_in = jnp.stack([grad_ins[1], grad_ins[2]])
    grad_mix_out = jnp.stack([grad_outs[1], grad_outs[2]])
    reduced = (
        lax.psum_scatter(grad_ffn_in, ("dp", "fsdp"), scatter_dimension=1, tiled=True),
        lax.psum_scatter(grad_ffn_out, ("dp", "fsdp"), scatter_dimension=1, tiled=True),
        lax.psum_scatter(grad_mix_in, ("dp", "fsdp"), scatter_dimension=1, tiled=True),
        lax.psum_scatter(grad_mix_out, ("dp", "fsdp"), scatter_dimension=1, tiled=True),
        lax.psum_scatter(grad_vectors, ("dp", "fsdp"), scatter_dimension=1, tiled=True),
    )
    sublayer_rms = jnp.sqrt(global_stats[:5] / (global_stats[5] * channels))
    masters = (ffn_in_master, ffn_out_master, mix_in_master, mix_out_master, vector_master)
    firsts = (ffn_in_first, ffn_out_first, mix_in_first, mix_out_first, vector_first)
    seconds = (ffn_in_second, ffn_out_second, mix_in_second, mix_out_second, vector_second)
    results = [
        adamw(
            masters[slot_index],
            firsts[slot_index],
            seconds[slot_index],
            reduced[slot_index],
            RATE_MATRIX if slot_index < 4 else RATE_VECTOR,
            WEIGHT_DECAY if slot_index < 4 else 0.0,
        )
        for slot_index in range(5)
    ]
    return (
        activations,
        grad_residual,
        results[0][0],
        results[1][0],
        results[2][0],
        results[3][0],
        results[4][0],
        results[0][1],
        results[1][1],
        results[2][1],
        results[3][1],
        results[4][1],
        results[0][2],
        results[1][2],
        results[2][2],
        results[3][2],
        results[4][2],
        results[0][3],
        results[1][3],
        results[2][3],
        results[3][3],
        results[4][3],
        sublayer_rms,
    )


def solution(mesh):
    return jax.shard_map(
        local,
        mesh=mesh,
        in_specs=(
            P(("dp", "fsdp"), None, None),
            P(("dp", "fsdp"), None, None),
            P(("dp", "fsdp")),
            P(None, ("dp", "fsdp"), None),
            P(None, ("dp", "fsdp"), None),
            P(None, ("dp", "fsdp"), None),
            P(None, ("dp", "fsdp"), None),
            P(None, ("dp", "fsdp")),
            P(None, ("dp", "fsdp"), None),
            P(None, ("dp", "fsdp"), None),
            P(None, ("dp", "fsdp"), None),
            P(None, ("dp", "fsdp"), None),
            P(None, ("dp", "fsdp")),
            P(None, ("dp", "fsdp"), None),
            P(None, ("dp", "fsdp"), None),
            P(None, ("dp", "fsdp"), None),
            P(None, ("dp", "fsdp"), None),
            P(None, ("dp", "fsdp")),
        ),
        out_specs=(
            P(("dp", "fsdp"), None, None),
            P(("dp", "fsdp"), None, None),
            P(None, ("dp", "fsdp"), None),
            P(None, ("dp", "fsdp"), None),
            P(None, ("dp", "fsdp"), None),
            P(None, ("dp", "fsdp"), None),
            P(None, ("dp", "fsdp")),
            P(None, ("dp", "fsdp"), None),
            P(None, ("dp", "fsdp"), None),
            P(None, ("dp", "fsdp"), None),
            P(None, ("dp", "fsdp"), None),
            P(None, ("dp", "fsdp")),
            P(None, ("dp", "fsdp"), None),
            P(None, ("dp", "fsdp"), None),
            P(None, ("dp", "fsdp"), None),
            P(None, ("dp", "fsdp"), None),
            P(None, ("dp", "fsdp")),
            P(None, ("dp", "fsdp"), None),
            P(None, ("dp", "fsdp"), None),
            P(None, ("dp", "fsdp"), None),
            P(None, ("dp", "fsdp"), None),
            P(None, ("dp", "fsdp")),
            P(),
        ),
        check_vma=False,
    )
```

profile of v0, /device:TPU:1, one launch (start us, length us, event | category | flops | bytes accessed | tf_op | source)
XLA Modules:
  0.0 1212.8 jit_solution(7263429991488102907)
XLA Ops:
  14.6 63.3 %all_gather.19 = bf16[30,512]{0,1:T(8,128)(2,1)S(1)} all-gather(bf16[30,16]{0,1:T(8,128)(2,1)S(1)} %convert_element_type.149), channel_id=1, replica_groups=mesh['dp'=4,'fsdp'=8] {'dp','fsdp'}, dimensions={1}, use_global_device_ids=true | all-gather | bytes 31680 | tf_op jit(solution)/shard_map/all_gather | solution.py:165
  84.3 6.0 slice.264
  90.3 12.6 %reshape.883 = f32[4190208]{0:T(1024)} reshape(f32[8,523776]{1,0:T(8,128)} %slice.264) | data formatting | bytes 33521664
  102.9 17.4 %reshape.848 = f32[8,512,1023]{2,1,0:T(8,128)} reshape(f32[4190208]{0:T(1024)} %reshape.883) | data formatting | bytes 33521664 | tf_op jit(solution)/shard_map/jvp()/reshape | solution.py:42
  120.3 5.0 fusion.11
  125.3 15.4 %all-gather.7.cloned.1.call-done = bf16[2,2048,512]{2,1,0:T(8,128)(2,1)} async-done(((bf16[2,64,512]{2,1,0:T(8,128)(2,1)}), bf16[2,2048,512]{2,1,0:T(8,128)(2,1)}) %all-gather.7.cloned.1.call-update) | async-done | bytes 4194320 | tf_op jit(solution)/shard_map/all_gather | solution.py:162
  140.6 5.4 fusion.139
  146.2 53.2 %all-gather.9.cloned.1.call-done = bf16[2,512,1024]{2,1,0:T(8,128)(2,1)} async-done(((bf16[2,16,1024]{2,1,0:T(8,128)(2,1)}), bf16[2,512,1024]{2,1,0:T(8,128)(2,1)}) %all-gather.9.cloned.1.call-update) | async-done | bytes 2097168 | tf_op jit(solution)/shard_map/all_gather | solution.py:163
  201.7 12.7 %fusion.2 = f32[8,64,512]{2,1,0:T(8,128)S(1)} fusion(f32[512,8,64]{0,2,1:T(8,128)S(1)} %bitcast.319, f32[8,512,1023]{2,1,0:T(8,128)} %reshape.848), kind=kOutput, calls=%fused_computation.4 | convolution fusion | flops 1610612736 | bytes 10485760 | tf_op jit(solution)/shard_map/jvp(hts,bshc->bthc)/dot_general | solution.py:59
  215.7 39.9 %all-gather.11.cloned.1.call-done = bf16[2,512,512]{2,1,0:T(8,128)(2,1)} async-done(((bf16[2,16,512]{2,1,0:T(8,128)(2,1)}), bf16[2,512,512]{2,1,0:T(8,128)(2,1)}) %all-gather.11.cloned.1.call-update) | async-done | bytes 1048592 | tf_op jit(solution)/shard_map/all_gather | solution.py:164
  261.0 5.6 fusion.137
  291.5 5.8 multiply_reduce_fusion.17
  298.9 3.1 pad_add_fusion
  315.5 9.4 fusion
  325.0 9.1 fusion.146
  343.8 4.4 fusion.9
  357.1 11.3 pad.212
  368.4 15.9 %reshape.885 = f32[4190208]{0:T(1024)} reshape(f32[8,512,1023]{2,1,0:T(8,128)} %pad.212) | data formatting | bytes 33521664
  384.3 16.4 %reshape.864 = f32[8,523776]{1,0:T(8,128)} reshape(f32[4190208]{0:T(1024)} %reshape.885) | data formatting | bytes 33521664 | tf_op jit(solution)/shard_map/transpose(jvp())/reshape | solution.py:42
  400.7 11.2 pad.213
  411.9 6.8 reduce_sum.638
  430.3 4.2 convolution_bitcast_fusion.1
  436.5 4.2 pad_maximum_fusion.1
  441.7 3.1 convolution_bitcast_fusion.3
  446.2 3.8 pad_maximum_fusion
  455.7 4.0 stack.75
  459.7 38.9 %psum.7 = f32[6]{0:T(128)S(1)} all-reduce(f32[6]{0:T(128)S(1)} %stack.75), channel_id=1, replica_groups=mesh['dp'=4,'fsdp'=8] {'dp','fsdp'}, use_global_device_ids=true, to_apply=%region_68.69 | all-reduce | flops 6 | bytes 48 | tf_op jit(solution)/shard_map/psum | solution.py:210
  506.7 38.8 %reduce-scatter.16.cloned.1.call-done = f32[16,30]{1,0:T(8,128)} async-done(((f32[512,30]{1,0:T(8,128)}), f32[16,30]{1,0:T(8,128)}) %reduce-scatter.16.cloned.1.call-update) | async-done | bytes 1936
  546.9 134.8 %reduce-scatter.14.cloned.1.call-done = f32[2,16,512]{2,1,0:T(8,128)} async-done(((f32[2,512,512]{2,1,0:T(8,128)}), f32[2,16,512]{2,1,0:T(8,128)}) %reduce-scatter.14.cloned.1.call-update) | async-done | bytes 65552 | tf_op jit(solution)/shard_map/reduce_scatter | solution.py:238
  683.4 143.7 %reduce-scatter.12.cloned.1.call-done = f32[2,16,1024]{2,1,0:T(8,128)} async-done(((f32[2,512,1024]{2,1,0:T(8,128)}), f32[2,16,1024]{2,1,0:T(8,128)}) %reduce-scatter.12.cloned.1.call-update) | async-done | bytes 131088 | tf_op jit(solution)/shard_map/reduce_scatter | solution.py:237
  829.0 188.5 %reduce-scatter.10.cloned.1.call-done = f32[2,64,512]{2,1,0:T(8,128)} async-done(((f32[2,2048,512]{2,1,0:T(8,128)}), f32[2,64,512]{2,1,0:T(8,128)}) %reduce-scatter.10.cloned.1.call-update) | async-done | bytes 262160 | tf_op jit(solution)/shard_map/reduce_scatter | solution.py:236
  1019.7 184.1 %reduce-scatter.8.cloned.1.call-done = f32[2,16,2048]{2,1,0:T(8,128)} async-done(((f32[2,512,2048]{2,1,0:T(8,128)}), f32[2,16,2048]{2,1,0:T(8,128)}) %reduce-scatter.8.cloned.1.call-update) | async-done | bytes 262160 | tf_op jit(solution)/shard_map/reduce_scatter | solution.py:235
  (279 shorter events, 117.7 us)
Async XLA Ops:
  7.2 73.9 %copy-start.50 = (bf16[1,512,512]{2,1,0:T(8,128)(2,1)S(1)}, bf16[1,512,512]{2,1,0:T(8,128)(2,1)}, u32[]{:S(2)}) copy-start(bf16[1,512,512]{2,1,0:T(8,128)(2,1)} %param.19) | copy-start | bytes 1572868
  7.2 113.1 %all-gather.5.cloned.1.call-start = ((), (), s32[]{:S(2)}) async-start(), calls=%async_computation.5 | async-start | bytes 4325376 | tf_op jit(solution)/shard_map/all_gather | solution.py:161
  8.9 131.7 %all-gather.7.cloned.1.call-start = ((), (), s32[]{:S(2)}) async-start(), calls=%async_computation.6 | async-start | bytes 4325376 | tf_op jit(solution)/shard_map/all_gather | solution.py:162
  10.6 188.8 %all-gather.9.cloned.1.call-start = ((), (), s32[]{:S(2)}) async-start(), calls=%async_computation.7 | async-start | bytes 2162688 | tf_op jit(solution)/shard_map/all_gather | solution.py:163
  12.3 243.3 %all-gather.11.cloned.1.call-start = ((), (), s32[]{:S(2)}) async-start(), calls=%async_computation.8 | async-start | bytes 1081344 | tf_op jit(solution)/shard_map/all_gather | solution.py:164
  13.8 531.7 %reduce-scatter.16.cloned.1.call-start = ((), (), s32[]{:S(2)}) async-start(), calls=%async_computation.13 | async-start | bytes 270336
  13.9 70.4 %copy-start.65 = (f32[512]{0:T(512)}, f32[512]{0:T(512)S(1)}, u32[]{:S(2)}) copy-start(f32[512]{0:T(512)S(1)} %iota_convert_fusion) | copy-start | bytes 6148
  78.1 42.2 %copy-start.63 = (f32[1,512]{1,0:T(1,128)}, f32[1,512]{1,0:T(1,128)S(1)}, u32[]{:S(2)}) copy-start(f32[1,512]{1,0:T(1,128)S(1)} %get-tuple-element.262) | copy-start | bytes 6148
  78.1 6.2 copy-start.57
  80.7 59.9 %copy-start.2 = (bf16[1,512,512]{1,2,0:T(8,128)(2,1)}, bf16[1,512,512]{1,2,0:T(8,128)(2,1)S(1)}, u32[]{:S(2)}) copy-start(bf16[1,512,512]{1,2,0:T(8,128)(2,1)S(1)} %copy.128) | copy-start | bytes 1572868
  201.5 12.8 %copy-start.9 = (f32[1,512,1024]{1,2,0:T(8,128)}, f32[1,512,1024]{1,2,0:T(8,128)S(1)}, u32[]{:S(2)}) copy-start(f32[1,512,1024]{1,2,0:T(8,128)S(1)} %convolution_bitcast_fusion.7) | copy-start | bytes 6291460
  201.7 12.7 %copy-start.11 = (f32[1,512,512]{1,2,0:T(8,128)}, f32[1,512,512]{1,2,0:T(8,128)S(1)}, u32[]{:S(2)}) copy-start(f32[1,512,512]{1,2,0:T(8,128)S(1)} %slice_multiply_fusion) | copy-start | bytes 3145732
  215.7 42.8 %copy-start.26 = (bf16[512,512]{0,1:T(8,128)(2,1)}, bf16[512,512]{0,1:T(8,128)(2,1)S(1)}, u32[]{:S(2)}) copy-start(bf16[512,512]{0,1:T(8,128)(2,1)S(1)} %fusion.58) | copy-start | bytes 1572868
  260.7 6.2 copy-start.54
  261.0 5.9 copy-start.16
  315.5 18.7 %copy-start.43 = (f32[1,512,512]{1,2,0:T(8,128)}, f32[1,512,512]{1,2,0:T(8,128)S(1)}, u32[]{:S(2)}) copy-start(f32[1,512,512]{1,2,0:T(8,128)S(1)} %get-tuple-element.212) | copy-start | bytes 3145732
  325.0 10.3 copy-start.42
  411.9 7.1 copy-start.60
  411.9 7.1 copy-start.62
  411.9 7.1 copy-start.66
  421.2 260.5 %reduce-scatter.14.cloned.1.call-start = ((), (), s32[]{:S(2)}) async-start(), calls=%async_computation.12 | async-start | bytes 2162688 | tf_op jit(solution)/shard_map/reduce_scatter | solution.py:238
  424.3 402.7 %reduce-scatter.12.cloned.1.call-start = ((), (), s32[]{:S(2)}) async-start(), calls=%async_computation.11 | async-start | bytes 4325376 | tf_op jit(solution)/shard_map/reduce_scatter | solution.py:237
  430.0 587.5 %reduce-scatter.10.cloned.1.call-start = ((), (), s32[]{:S(2)}) async-start(), calls=%async_computation.10 | async-start | bytes 8650752 | tf_op jit(solution)/shard_map/reduce_scatter | solution.py:236
  440.7 763.1 %reduce-scatter.8.cloned.1.call-start = ((), (), s32[]{:S(2)}) async-start(), calls=%async_computation.9 | async-start | bytes 8650752 | tf_op jit(solution)/shard_map/reduce_scatter | solution.py:235
  450.0 51.9 %copy-start.58 = (f32[512]{0:T(512)S(1)}, f32[512]{0:T(512)}, u32[]{:S(2)}) copy-start(f32[512]{0:T(512)} %get-tuple-element.164) | copy-start | bytes 6148
  450.0 51.9 %copy-start.4 = (f32[512,512]{0,1:T(8,128)S(1)}, f32[512,512]{0,1:T(8,128)}, u32[]{:S(2)}) copy-start(f32[512,512]{0,1:T(8,128)} %copy.137) | copy-start | bytes 3145732
  499.2 327.9 %copy-start.49 = (f32[2,16,1024]{2,1,0:T(8,128)S(1)}, f32[2,16,1024]{2,1,0:T(8,128)}, u32[]{:S(2)}) copy-start(f32[2,16,1024]{2,1,0:T(8,128)} %param.23) | copy-start | bytes 393220
  499.2 518.3 %copy-start.45 = (f32[2,64,512]{2,1,0:T(8,128)S(1)}, f32[2,64,512]{2,1,0:T(8,128)}, u32[]{:S(2)}) copy-start(f32[2,64,512]{2,1,0:T(8,128)} %param.22) | copy-start | bytes 786436
  499.2 518.3 %copy-start.51 = (f32[2,64,512]{2,1,0:T(8,128)S(1)}, f32[2,64,512]{2,1,0:T(8,128)}, u32[]{:S(2)}) copy-start(f32[2,64,512]{2,1,0:T(8,128)} %param.27) | copy-start | bytes 786436
  501.9 701.9 %copy-start.46 = (f32[2,16,2048]{2,1,0:T(8,128)S(1)}, f32[2,16,2048]{2,1,0:T(8,128)}, u32[]{:S(2)}) copy-start(f32[2,16,2048]{2,1,0:T(8,128)} %param.21) | copy-start | bytes 786436
  503.5 700.3 %copy-start.52 = (f32[2,16,2048]{2,1,0:T(8,128)S(1)}, f32[2,16,2048]{2,1,0:T(8,128)}, u32[]{:S(2)}) copy-start(f32[2,16,2048]{2,1,0:T(8,128)} %param.26) | copy-start | bytes 786436
  503.5 700.3 %copy-start.53 = (f32[2,16,2048]{2,1,0:T(8,128)S(1)}, f32[2,16,2048]{2,1,0:T(8,128)}, u32[]{:S(2)}) copy-start(f32[2,16,2048]{2,1,0:T(8,128)} %param.31) | copy-start | bytes 786436
  (48 other events, 138.4 us)
Sparse Core Ops, SparseCore 0:
  11.7 64.6 all-gather.4
  80.0 60.5 all-gather.6
  144.3 55.1 all-gather.8
  202.9 52.6 all-gather.10
  421.4 124.1 reduce-scatter.15
  547.7 133.9 reduce-scatter.13
  684.0 143.0 reduce-scatter.11
  829.4 188.0 reduce-scatter.9
  1019.8 183.9 reduce-scatter.7
where the time goes:
time: 1220 us; the launch traced here: 1210 us
  waiting for transfers between devices  799 us (65%)
  local copies, waits for them, and re-layouts  123 us (10%)
  blocking collectives  102 us (8%)
  matrix products  86.7 us (7%)
  other arithmetic  84.8 us (7%)
  between operations  17 us (1%)
    reduce_scatter x1, waiting for transfers between devices, local(): lax.psum_scatter(grad_ffn_out, ('dp', 'fsdp'), scatter_dimension=1, tiled...  189 us
    reduce_scatter x1, waiting for transfers between devices, local(): lax.psum_scatter(grad_ffn_in, ('dp', 'fsdp'), scatter_dimension=1, tiled=...  184 us
    reduce_scatter x1, waiting for transfers between devices, local(): lax.psum_scatter(grad_mix_in, ('dp', 'fsdp'), scatter_dimension=1, tiled=...  144 us
    reduce_scatter x1, waiting for transfers between devices, local(): lax.psum_scatter(grad_mix_out, ('dp', 'fsdp'), scatter_dimension=1, tiled...  135 us
    all_gather x1, blocking collectives, local(): lax.all_gather(vector_low, ('dp', 'fsdp'), axis=1, tiled=True)  63.3 us
    all_gather x1, waiting for transfers between devices, local(): lax.all_gather(mix_in_low, ('dp', 'fsdp'), axis=1, tiled=True)  53.2 us
    unnamed x149, local copies, waits for them, and re-layouts  42.6 us
    all_gather x1, waiting for transfers between devices, local(): lax.all_gather(mix_out_low, ('dp', 'fsdp'), axis=1, tiled=True)  39.9 us
  transfers between devices with their start and end apart: 9, of which 8 were waited for; matrix products, arithmetic and copies ran while one was open for 10% of the time, Pallas kernels for 0%

commit v1 on v0

--- a/solution.py
+++ b/solution.py
@@ -1,4 +1,5 @@
 import jax
+import numpy as np
 import jax.numpy as jnp
 from jax import lax
 from jax.sharding import PartitionSpec as P
@@ -129,6 +130,85 @@
     grad_normed = inner_cols(grad_proj_low, weight_in).reshape(seq_count, length, channels)
     grad_residual, grad_vec_norm = pull_norm(grad_normed)
     return (grad_residual, grad_in_weight, grad_out_weight, grad_vec_local + grad_vec_norm)
+
+
+def piece_tables():
+    tables = []
+    for me in range(32):
+        core = (me >> 3) & 1
+        pieces = []
+        for side in (0, 1):
+            base = me ^ (8 * side)
+            across = ((16, 1), (1, 16))[core ^ side]
+            for spot in range(16):
+                rel = (across[0] if spot & 8 else 0) | (across[1] if spot & 4 else 0)
+                rel |= (2 if spot & 2 else 0) | (4 if spot & 1 else 0)
+                pieces.append(base ^ rel)
+        tables.append(pieces)
+    return np.array(tables, np.int32)
+
+
+TABLES = piece_tables()
+SPOTS = np.argsort(TABLES, axis=1).astype(np.int32)
+AXES = ("dp", "fsdp")
+CORE, Z_HIGH, Z_LOW = 8, 4, 2
+STAGES = (Z_HIGH, Z_LOW, (1, 16), (16, 1))
+
+
+def swap(values, mask):
+    masks = mask if isinstance(mask, tuple) else (mask, mask)
+    return lax.ppermute(values, AXES, [(i, i ^ masks[(i >> 3) & 1]) for i in range(32)])
+
+
+def gather_pieces(shard, extra=None):
+    rows = shard.shape[0]
+    held = shard[None]
+    for mask in STAGES + (CORE,):
+        if extra is None:
+            got = swap(held, mask)
+        else:
+            sent = jnp.concatenate([held.reshape(-1, 512), extra])
+            got = swap(sent, mask)
+            extra = extra + got[-extra.shape[0] :]
+            got = got[: -extra.shape[0]].reshape(held.shape)
+        if mask != CORE:
+            held = jnp.concatenate([held, got])
+    return held, got, extra
+
+
+def reduce_pieces(kept, sent):
+    got = swap(sent, CORE)
+    half = 8
+    for mask in STAGES[::-1]:
+        sent = (kept[half:].astype(jnp.float32) + got[half:].astype(jnp.float32)).astype(jnp.bfloat16)
+        new = swap(sent, mask)
+        kept = (kept[:half].astype(jnp.float32) + got[:half].astype(jnp.float32)).astype(jnp.bfloat16)
+        got = new
+        half //= 2
+    return (kept[0].astype(jnp.float32) + got[0].astype(jnp.float32))
+
+
+def sum_all(values):
+    for mask in (CORE,) + STAGES[::-1]:
+        values = values + swap(values, mask)
+    return values
+
+
+def cut_columns(matrix):
+    rows, columns = matrix.shape
+    return matrix.reshape(rows, columns // 512, 512).transpose(1, 0, 2).reshape(-1, 512)
+
+
+def pieces_of(matrix):
+    by_piece = matrix.reshape(32, matrix.shape[0] // 32, -1, 512)
+    return jnp.moveaxis(by_piece, 2, 1).reshape(32, -1, 512)
+
+
+def join_columns(pieces, columns):
+    lead = pieces.shape[:-2]
+    rows = pieces.shape[-2] // columns
+    moved = jnp.moveaxis(pieces.reshape(*lead, columns, rows, 512), -3, -2)
+    return moved.reshape(*lead, rows, columns * 512)
 
 
 def local(
@@ -152,17 +232,52 @@
     vector_second,
 ):
     seq_count, length, channels = frames.shape
-    ffn_in_low = ffn_in_master.astype(jnp.bfloat16)
-    ffn_out_low = ffn_out_master.astype(jnp.bfloat16)
-    mix_in_low = mix_in_master.astype(jnp.bfloat16)
-    mix_out_low = mix_out_master.astype(jnp.bfloat16)
-    vector_low = vector_master.astype(jnp.bfloat16)
+    me = lax.axis_index(AXES)
+    paired = (lax.axis_size("dp"), lax.axis_size("fsdp")) == (4, 8)
+    spots = jnp.asarray(SPOTS)[me] if paired else jnp.arange(32)
+    table = jnp.asarray(TABLES)[me] if paired else jnp.arange(32)
+    low = jnp.bfloat16
+
+    def pack(parts):
+        return jnp.concatenate([cut_columns(part.astype(low)) for part in parts])
+
+    def gather(parts, extra=None):
+        if paired:
+            return gather_pieces(pack(parts), extra)
+        gathered = [lax.all_gather(part.astype(low), AXES, axis=0, tiled=True) for part in parts]
+        pieces = jnp.concatenate([pieces_of(matrix) for matrix in gathered], axis=1)
+        return pieces[:16], pieces[16:], None if extra is None else lax.psum(extra, AXES)
+
+    def reduce(matrices):
+        pieces = jnp.concatenate([pieces_of(matrix.astype(low)) for matrix in matrices], axis=1)
+        if paired:
+            pieces = jnp.take(pieces, table, axis=0)
+            return reduce_pieces(pieces[:16], pieces[16:])
+        sums = [lax.psum_scatter(m, AXES, scatter_dimension=0, tiled=True) for m in matrices]
+        return jnp.concatenate([cut_columns(part) for part in sums])
+
+    total = sum_all if paired else lambda values: lax.psum(values, AXES)
+    width = vector_master.shape[1]
+    placed = lax.dynamic_update_slice(
+        jnp.zeros((32, 512), low), vector_master.astype(low), (0, width * me)
+    )
+    own0, other0, placed = gather([ffn_in_master[0], ffn_out_master[0]], placed)
+    own1, other1, _ = gather([mix_in_master[0], mix_out_master[0], mix_in_master[1], mix_out_master[1]])
+    own2, other2, _ = gather([ffn_in_master[1], ffn_out_master[1]])
+
+    def natural(own, other):
+        return jnp.take(jnp.concatenate([own, other]), spots, axis=0)
+
+    def whole(pieces, columns):
+        return join_columns(pieces, columns).reshape(-1, 512 * columns)
+
+    nat0, nat1, nat2 = natural(own0, other0), natural(own1, other1), natural(own2, other2)
     gathered = (
-        lax.all_gather(ffn_in_low, ("dp", "fsdp"), axis=1, tiled=True),
-        lax.all_gather(ffn_out_low, ("dp", "fsdp"), axis=1, tiled=True),
-        lax.all_gather(mix_in_low, ("dp", "fsdp"), axis=1, tiled=True),
-        lax.all_gather(mix_out_low, ("dp", "fsdp"), axis=1, tiled=True),
-        lax.all_gather(vector_low, ("dp", "fsdp"), axis=1, tiled=True),
+        (whole(nat0[:, :64], 4), whole(nat2[:, :64], 4)),
+        (whole(nat0[:, 64:], 1), whole(nat2[:, 64:], 1)),
+        (whole(nat1[:, :32], 2), whole(nat1[:, 48:80], 2)),
+        (whole(nat1[:, 32:48], 1), whole(nat1[:, 80:96], 1)),
+        placed[:30],
     )
     vectors = gathered[4].astype(jnp.float32)
     positions = jnp.arange(length, dtype=jnp.int32)
@@ -207,15 +322,9 @@
     piece_outs.append(residual)
     squares = [jnp.sum(valid * piece_out * piece_out) for piece_out in piece_outs]
     local_stats = jnp.stack(squares + [jnp.sum(valid)])
-    global_stats = lax.psum(local_stats, ("dp", "fsdp"))
+    global_stats = total(jnp.pad(local_stats, (0, 122))[None] * jnp.ones((8, 1)))[0]
     grad_residual, grad_vectors = pull_final(cotangent.astype(jnp.float32))
-    back_weights = (
-        lax.all_gather(ffn_in_low, ("dp", "fsdp"), axis=1, tiled=True),
-        lax.all_gather(ffn_out_low, ("dp", "fsdp"), axis=1, tiled=True),
-        lax.all_gather(mix_in_low, ("dp", "fsdp"), axis=1, tiled=True),
-        lax.all_gather(mix_out_low, ("dp", "fsdp"), axis=1, tiled=True),
-        lax.all_gather(vector_low, ("dp", "fsdp"), axis=1, tiled=True),
-    )
+    back_weights = gathered
     grad_ins = [None, None, None, None]
     grad_outs = [None, None, None, None]
     for module in (3, 2, 1, 0):
@@ -227,16 +336,17 @@
         grad_vectors = grad_vectors + grad_vec_more
         grad_ins[module] = grad_in_weight
         grad_outs[module] = grad_out_weight
-    grad_ffn_in = jnp.stack([grad_ins[0], grad_ins[3]])
-    grad_ffn_out = jnp.stack([grad_outs[0], grad_outs[3]])
-    grad_mix_in = jnp.stack([grad_ins[1], grad_ins[2]])
-    grad_mix_out = jnp.stack([grad_outs[1], grad_outs[2]])
+    sum2 = reduce([grad_ins[3], grad_outs[3]])
+    sum1 = reduce([grad_ins[1], grad_outs[1], grad_ins[2], grad_outs[2]])
+    sum0 = reduce([grad_ins[0], grad_outs[0]])
+    all_vectors = total(jnp.pad(grad_vectors, ((0, 2), (0, 0))))
+    n = ffn_in_master.shape[1]
     reduced = (
-        lax.psum_scatter(grad_ffn_in, ("dp", "fsdp"), scatter_dimension=1, tiled=True),
-        lax.psum_scatter(grad_ffn_out, ("dp", "fsdp"), scatter_dimension=1, tiled=True),
-        lax.psum_scatter(grad_mix_in, ("dp", "fsdp"), scatter_dimension=1, tiled=True),
-        lax.psum_scatter(grad_mix_out, ("dp", "fsdp"), scatter_dimension=1, tiled=True),
-        lax.psum_scatter(grad_vectors, ("dp", "fsdp"), scatter_dimension=1, tiled=True),
+        jnp.stack([join_columns(sum0[: 4 * n], 4), join_columns(sum2[: 4 * n], 4)]),
+        jnp.stack([sum0[4 * n :], sum2[4 * n :]]),
+        jnp.stack([join_columns(sum1[: 2 * n], 2), join_columns(sum1[3 * n : 5 * n], 2)]),
+        jnp.stack([sum1[2 * n : 3 * n], sum1[5 * n :]]),
+        lax.dynamic_slice(all_vectors, (0, width * me), (30, width)),
     )
     sublayer_rms = jnp.sqrt(global_stats[:5] / (global_stats[5] * channels))
     masters = (ffn_in_master, ffn_out_master, mix_in_master, mix_out_master, vector_master)

time: 1220 us -> 604 us (0.50)
  waiting for transfers between devices: 799 us -> 94.5 us
  local copies, waits for them, and re-layouts: 123 us -> 268 us
  blocking collectives: 102 us -> 0 us
  starting transfers between devices: 0.62 us -> 37.4 us
  other arithmetic: 84.8 us -> 113 us
  between operations: 17 us -> 4.07 us
    reduce_scatter x4 -> x0, waiting for transfers between devices: 651 us -> none  [the longest x1 189 us: local(): lax.psum_scatter(grad_ffn_out, ('dp', 'fsdp'), scatter_dimension=1, tiled...]
    all_gather x4 -> x0, waiting for transfers between devices: 108 us -> none  [the longest x1 53.2 us: local(): lax.all_gather(mix_in_low, ('dp', 'fsdp'), axis=1, tiled=True)]
    ppermute x0 -> x40, waiting for transfers between devices: none -> 94.5 us  [swap(): lax.ppermute(values, AXES, [(i, i ^ masks[i >> 3 & 1]) for i in range(32)])]
    all_gather x1 -> x0, blocking collectives: 63.3 us -> none  [local(): lax.all_gather(vector_low, ('dp', 'fsdp'), axis=1, tiled=True)]
    unnamed x10 -> x0, waiting for transfers between devices: 39 us -> none
    psum x1 -> x0, blocking collectives: 38.9 us -> none  [local(): global_stats = lax.psum(local_stats, ('dp', 'fsdp'))]
    ppermute x0 -> x40, starting transfers between devices: none -> 37.4 us  [swap(): lax.ppermute(values, AXES, [(i, i ^ masks[i >> 3 & 1]) for i in range(32)])]
    gather x0 -> x6, local copies, waits for them, and re-layouts: none -> 29.7 us  [the longest x3 15 us: natural(): return jnp.take(jnp.concatenate([own, other]), spots, axis=0)]
  transfers between devices with their start and end apart: 9 -> 40, of which waited for: 8 -> 16; matrix products, arithmetic and copies ran while one was open for 10% -> 44% of each run, Pallas kernels for 0% -> 0%
where the time goes in v1:
time: 604 us; the launch traced here: 592 us
  local copies, waits for them, and re-layouts  268 us (44%)
  other arithmetic  113 us (19%)
  waiting for transfers between devices  94.5 us (16%)
  matrix products  75.8 us (13%)
  starting transfers between devices  37.4 us (6%)
    ppermute x40, waiting for transfers between devices, swap(): lax.ppermute(values, AXES, [(i, i ^ masks[i >> 3 & 1]) for i in range(32)])  94.5 us
    unnamed x249, local copies, waits for them, and re-layouts  64 us
    ppermute x40, starting transfers between devices, swap(): lax.ppermute(values, AXES, [(i, i ^ masks[i >> 3 & 1]) for i in range(32)])  37.4 us
    reshape x2, local copies, waits for them, and re-layouts, causal_toeplitz(): repeated[:, :length * (2 * length - 1)]  33.7 us
    dot_general x3, matrix products, long_conv(): jnp.einsum('hts,bshc->bthc', toeplitz, by_head, precision=HIGHEST)  28.6 us
    reshape x8, local copies, waits for them, and re-layouts, pieces_of(): by_piece = matrix.reshape(32, matrix.shape[0] // 32, -1, 512)  17 us
    dot_general x8, matrix products, inner_rows(): lax.dot_general(left_side, right_side, (((0,), (0,)), ((), ())), preferre...  16.5 us
    dot_general x8, matrix products, matmul(): return jnp.dot(left_side, right_side, preferred_element_type=jnp.float32)  15.6 us
  transfers between devices with their start and end apart: 40, of which 16 were waited for; matrix products, arithmetic and copies ran while one was open for 44% of the time, Pallas kernels for 0%

profile of v1, /device:TPU:1, one launch (start us, length us, event | category | flops | bytes accessed | tf_op | source)
XLA Modules:
  0.0 592.1 jit_solution(3575659430484041437)
XLA Ops:
  21.6 6.3 %collective-permute-done.10 = bf16[1,128,512]{1,2,0:T(8,128)(2,1)S(1)} collective-permute-done((bf16[1,128,512]{1,2,0:T(8,128)(2,1)S(1)}, bf16[1,128,512]{1,2,0:T(8,128)(2,1)S(1)}, u32[]{:S(2)}, u32[]{:S(2)}) %collective-permute-start.10) | collective-permute-done | bytes 131104 | tf_op jit(solution)/shard_map/ppermute | solution.py:160
  40.5 6.3 %collective-permute-done.1 = bf16[288,512]{0,1:T(8,128)(2,1)S(1)} collective-permute-done((bf16[288,512]{0,1:T(8,128)(2,1)S(1)}, bf16[288,512]{0,1:T(8,128)(2,1)S(1)}, u32[]{:S(2)}, u32[]{:S(2)}) %collective-permute-start.1) | collective-permute-done | bytes 294944 | tf_op jit(solution)/shard_map/ppermute | solution.py:160
  65.1 4.3 collective-permute-done.8
  74.7 5.9 collective-permute-done.13
  99.6 4.5 gather_fusion.1
  115.4 5.4 gather_fusion.2
  127.6 4.8 copy.307
  148.6 5.1 gather_fusion
  170.4 6.0 %slice.631 = f32[8,523776]{1,0:T(8,128)} slice(f32[8,524288]{1,0:T(8,128)S(1)} %bitcast.339), slice={[0:8], [0:523776]} | slice | bytes 33521664 | tf_op jit(solution)/shard_map/jvp()/slice | solution.py:43
  176.4 12.6 %reshape.1141 = f32[4190208]{0:T(1024)} reshape(f32[8,523776]{1,0:T(8,128)} %slice.631) | data formatting | bytes 33521664
  188.9 17.3 %reshape.1007 = f32[8,512,1023]{2,1,0:T(8,128)} reshape(f32[4190208]{0:T(1024)} %reshape.1141) | data formatting | bytes 33521664 | tf_op jit(solution)/shard_map/jvp()/reshape | solution.py:43
  207.2 12.7 %fusion.2 = f32[8,64,512]{2,1,0:T(8,128)S(1)} fusion(f32[512,8,64]{0,2,1:T(8,128)S(1)} %bitcast.340, f32[8,512,1023]{2,1,0:T(8,128)} %reshape.1007), kind=kOutput, calls=%fused_computation.8 | convolution fusion | flops 1610612736 | bytes 10485760 | tf_op jit(solution)/shard_map/jvp(hts,bshc->bthc)/dot_general | solution.py:60
  225.6 5.4 fusion.141
  260.9 5.8 multiply_reduce_fusion.17
  287.2 9.2 %fusion = f32[8,64,512]{2,1,0:T(8,128)S(1)} fusion(f32[8,64,512]{2,1,0:T(8,128)S(1)} %bitcast.342, f32[8,512,1023]{2,1,0:T(8,128)} %reshape.1007), kind=kOutput, calls=%fused_computation.6 | convolution fusion | flops 1610612736 | bytes 10485760 | tf_op jit(solution)/shard_map/transpose(jvp(hts,bshc->bthc))/dot_general | solution.py:60
  359.1 5.2 gather_fusion.4
  367.1 4.4 gather_fusion.5
  380.6 5.1 gather_fusion.3
  406.4 6.7 %fusion.158 = f32[8,512,512]{2,1,0:T(8,128)S(1)} fusion(f32[8,64,512]{2,1,0:T(8,128)S(1)} %bitcast.343, f32[512,8,64]{0,2,1:T(8,128)S(1)} %bitcast.341), kind=kOutput, calls=%fused_computation.458 | convolution fusion | flops 1610612736 | bytes 10485760 | tf_op jit(solution)/shard_map/transpose(jvp(hts,bshc->bthc))/dot_general | solution.py:60
  413.1 7.5 %pad.220 = f32[8,512,1023]{2,1,0:T(8,128)} pad(f32[8,512,512]{2,1,0:T(8,128)S(1)} %fusion.158, f32[]{:T(128)} %constant.60.clone.1), padding=0_0x0_0x511_0 | pad | bytes 25149444 | tf_op jit(solution)/shard_map/transpose(jvp())/pad | solution.py:44
  420.6 16.1 %reshape.1143 = f32[4190208]{0:T(1024)} reshape(f32[8,512,1023]{2,1,0:T(8,128)} %pad.220) | data formatting | bytes 33521664
  436.7 16.4 %reshape.1038 = f32[8,523776]{1,0:T(8,128)} reshape(f32[4190208]{0:T(1024)} %reshape.1143) | data formatting | bytes 33521664 | tf_op jit(solution)/shard_map/transpose(jvp())/reshape | solution.py:43
  453.0 11.2 %pad.221 = f32[8,524288]{1,0:T(8,128)} pad(f32[8,523776]{1,0:T(8,128)} %reshape.1038, f32[]{:T(128)} %constant.60.clone.1), padding=0_0x0_512 | pad | bytes 33538052 | tf_op jit(solution)/shard_map/transpose(jvp())/pad | solution.py:43
  464.3 6.9 %reduce_sum.638 = f32[8,1024]{1,0:T(8,128)S(1)} reduce(f32[8,512,1024]{2,0,1:T(8,128)} %bitcast.338, f32[]{:T(128)} %constant.60.clone.1), dimensions={1}, to_apply=%region_50.53 | reduce | flops 4186112 | bytes 16809988 | tf_op jit(solution)/shard_map/transpose(jvp())/reduce_sum | solution.py:40
  478.9 4.8 add_add_fusion.10
  492.0 9.9 %collective-permute-done.31 = f32[32,512]{0,1:T(8,128)S(1)} collective-permute-done((f32[32,512]{0,1:T(8,128)S(1)}, f32[32,512]{0,1:T(8,128)S(1)}, u32[]{:S(2)}, u32[]{:S(2)}) %collective-permute-start.31) | collective-permute-done | bytes 65568 | tf_op jit(solution)/shard_map/ppermute | solution.py:160
  511.8 5.5 collective-permute-done.33
  521.1 10.3 %collective-permute-done.34 = f32[32,512]{0,1:T(8,128)S(1)} collective-permute-done((f32[32,512]{0,1:T(8,128)S(1)}, f32[32,512]{0,1:T(8,128)S(1)}, u32[]{:S(2)}, u32[]{:S(2)}) %collective-permute-start.34) | collective-permute-done | bytes 65568 | tf_op jit(solution)/shard_map/ppermute | solution.py:160
  543.8 6.6 %collective-permute-done.16 = bf16[8,128,512]{2,1,0:T(8,128)(2,1)S(1)} collective-permute-done((bf16[8,128,512]{2,1,0:T(8,128)(2,1)}, bf16[8,128,512]{2,1,0:T(8,128)(2,1)S(1)}, u32[]{:S(2)}, u32[]{:S(2)}) %collective-permute-start.16) | collective-permute-done | bytes 1048608 | tf_op jit(solution)/shard_map/ppermute | solution.py:160
  550.7 16.3 %collective-permute-done.21 = bf16[8,128,512]{2,1,0:T(8,128)(2,1)} collective-permute-done((bf16[8,128,512]{2,1,0:T(8,128)(2,1)}, bf16[8,128,512]{2,1,0:T(8,128)(2,1)}, u32[]{:S(2)}, u32[]{:S(2)}) %collective-permute-start.21) | collective-permute-done | bytes 1048608 | tf_op jit(solution)/shard_map/ppermute | solution.py:160
  570.8 6.2 %collective-permute-done.22 = bf16[4,128,512]{2,1,0:T(8,128)(2,1)S(1)} collective-permute-done((bf16[4,128,512]{2,1,0:T(8,128)(2,1)S(1)}, bf16[4,128,512]{2,1,0:T(8,128)(2,1)S(1)}, u32[]{:S(2)}, u32[]{:S(2)}) %collective-permute-start.22) | collective-permute-done | bytes 524320 | tf_op jit(solution)/shard_map/ppermute | solution.py:160
  585.0 4.3 collective-permute-done.24
  (600 shorter events, 333.1 us)
Async XLA Ops:
  2.6 17.0 %collective-permute-start.5 = (bf16[1,96,512]{2,1,0:T(8,128)(2,1)S(1)}, bf16[1,96,512]{2,1,0:T(8,128)(2,1)S(1)}, u32[]{:S(2)}, u32[]{:S(2)}) collective-permute-start(bf16[1,96,512]{2,1,0:T(8,128)(2,1)S(1)} %maximum_bitcast_fusion.2), channel_id=1, source_target_pairs={{0,4},{1,5},{2,6},{3,7},{4,0},{5,1},{6,2},{7,3},{8,12},{9,13},{10,... | collective-permute-start | bytes 294920 | tf_op jit(solution)/shard_map/ppermute | solution.py:160
  8.5 20.8 %collective-permute-start = (bf16[160,512]{0,1:T(8,128)(2,1)S(1)}, bf16[160,512]{0,1:T(8,128)(2,1)S(1)}, u32[]{:S(2)}, u32[]{:S(2)}) collective-permute-start(bf16[160,512]{0,1:T(8,128)(2,1)S(1)} %pad_maximum_fusion.13), channel_id=1, source_target_pairs={{0,4},{1,5},{2,6},{3,7},{4,0},{5,1},{6,2},{7,3},{8,12},{9,13},{10,... | collective-permute-start | bytes 491528 | tf_op jit(solution)/shard_map/ppermute | solution.py:160
  9.5 18.4 %collective-permute-start.10 = (bf16[1,128,512]{1,2,0:T(8,128)(2,1)S(1)}, bf16[1,128,512]{1,2,0:T(8,128)(2,1)S(1)}, u32[]{:S(2)}, u32[]{:S(2)}) collective-permute-start(bf16[1,128,512]{1,2,0:T(8,128)(2,1)S(1)} %get-tuple-element.264), channel_id=1, source_target_pairs={{0,4},{1,5},{2,6},{3,7},{4,0},{5,1},{6,2},{7,3},{8,12},{9,13},{10,... | collective-permute-start | bytes 393224 | tf_op jit(solution)/shard_map/ppermute | solution.py:160
  20.3 12.9 %collective-permute-start.6 = (bf16[2,96,512]{2,1,0:T(8,128)(2,1)}, bf16[2,96,512]{2,1,0:T(8,128)(2,1)S(1)}, u32[]{:S(2)}, u32[]{:S(2)}) collective-permute-start(bf16[2,96,512]{2,1,0:T(8,128)(2,1)} %pad_maximum_fusion.17), channel_id=1, source_target_pairs={{0,2},{1,3},{2,0},{3,1},{4,6},{5,7},{6,4},{7,5},{8,10},{9,11},{10,... | collective-permute-start | bytes 589832 | tf_op jit(solution)/shard_map/ppermute | solution.py:160
  28.6 9.9 %collective-permute-start.11 = (bf16[2,128,512]{1,2,0:T(8,128)(2,1)}, bf16[2,128,512]{1,2,0:T(8,128)(2,1)S(1)}, u32[]{:S(2)}, u32[]{:S(2)}) collective-permute-start(bf16[2,128,512]{1,2,0:T(8,128)(2,1)} %pad_maximum_fusion.15), channel_id=1, source_target_pairs={{0,2},{1,3},{2,0},{3,1},{4,6},{5,7},{6,4},{7,5},{8,10},{9,11},{10,... | collective-permute-start | bytes 786440 | tf_op jit(solution)/shard_map/ppermute | solution.py:160
  30.3 16.5 %collective-permute-start.1 = (bf16[288,512]{0,1:T(8,128)(2,1)S(1)}, bf16[288,512]{0,1:T(8,128)(2,1)S(1)}, u32[]{:S(2)}, u32[]{:S(2)}) collective-permute-start(bf16[288,512]{0,1:T(8,128)(2,1)S(1)} %pad_maximum_fusion.11), channel_id=1, source_target_pairs={{0,2},{1,3},{2,0},{3,1},{4,6},{5,7},{6,4},{7,5},{8,10},{9,11},{10,... | collective-permute-start | bytes 884744 | tf_op jit(solution)/shard_map/ppermute | solution.py:160
  33.9 19.4 %collective-permute-start.7 = (bf16[4,96,512]{2,1,0:T(8,128)(2,1)}, bf16[4,96,512]{2,1,0:T(8,128)(2,1)}, u32[]{:S(2)}, u32[]{:S(2)}) collective-permute-start(bf16[4,96,512]{2,1,0:T(8,128)(2,1)} %pad_maximum_fusion.12), channel_id=1, source_target_pairs={{0,1},{1,0},{2,3},{3,2},{4,5},{5,4},{6,7},{7,6},{8,24},{9,25},{10,... | collective-permute-start | bytes 1179656 | tf_op jit(solution)/shard_map/ppermute | solution.py:160
  39.3 18.2 %collective-permute-start.12 = (bf16[4,128,512]{1,2,0:T(8,128)(2,1)}, bf16[4,128,512]{1,2,0:T(8,128)(2,1)S(1)}, u32[]{:S(2)}, u32[]{:S(2)}) collective-permute-start(bf16[4,128,512]{1,2,0:T(8,128)(2,1)} %pad_maximum_fusion.10), channel_id=1, source_target_pairs={{0,1},{1,0},{2,3},{3,2},{4,5},{5,4},{6,7},{7,6},{8,24},{9,25},{10,... | collective-permute-start | bytes 1572872 | tf_op jit(solution)/shard_map/ppermute | solution.py:160
  50.6 10.2 %collective-permute-start.2 = (bf16[544,512]{1,0:T(8,128)(2,1)}, bf16[544,512]{1,0:T(8,128)(2,1)S(1)}, u32[]{:S(2)}, u32[]{:S(2)}) collective-permute-start(bf16[544,512]{1,0:T(8,128)(2,1)} %pad_maximum_fusion.8), channel_id=1, source_target_pairs={{0,1},{1,0},{2,3},{3,2},{4,5},{5,4},{6,7},{7,6},{8,24},{9,25},{10,... | collective-permute-start | bytes 1671176 | tf_op jit(solution)/shard_map/ppermute | solution.py:160
  55.3 14.1 %collective-permute-start.8 = (bf16[8,96,512]{2,1,0:T(8,128)(2,1)}, bf16[8,96,512]{2,1,0:T(8,128)(2,1)}, u32[]{:S(2)}, u32[]{:S(2)}) collective-permute-start(bf16[8,96,512]{2,1,0:T(8,128)(2,1)} %pad_maximum_fusion.7), channel_id=1, source_target_pairs={{0,16},{1,17},{2,18},{3,19},{4,20},{5,21},{6,22},{7,23},{8,9},{9,8... | collective-permute-start | bytes 2359304 | tf_op jit(solution)/shard_map/ppermute | solution.py:160
  58.6 22.0 %collective-permute-start.13 = (bf16[8,128,512]{1,2,0:T(8,128)(2,1)}, bf16[8,128,512]{1,2,0:T(8,128)(2,1)}, u32[]{:S(2)}, u32[]{:S(2)}) collective-permute-start(bf16[8,128,512]{1,2,0:T(8,128)(2,1)} %pad_maximum_fusion.6), channel_id=1, source_target_pairs={{0,16},{1,17},{2,18},{3,19},{4,20},{5,21},{6,22},{7,23},{8,9},{9,8... | collective-permute-start | bytes 3145736 | tf_op jit(solution)/shard_map/ppermute | solution.py:160
  63.8 28.1 %collective-permute-start.3 = (bf16[1056,512]{1,0:T(8,128)(2,1)}, bf16[1056,512]{1,0:T(8,128)(2,1)}, u32[]{:S(2)}, u32[]{:S(2)}) collective-permute-start(bf16[1056,512]{1,0:T(8,128)(2,1)} %pad_maximum_fusion.4), channel_id=1, source_target_pairs={{0,16},{1,17},{2,18},{3,19},{4,20},{5,21},{6,22},{7,23},{8,9},{9,8... | collective-permute-start | bytes 3244040 | tf_op jit(solution)/shard_map/ppermute | solution.py:160
  71.9 25.0 %collective-permute-start.9 = (bf16[16,96,512]{2,1,0:T(8,128)(2,1)}, bf16[16,96,512]{2,1,0:T(8,128)(2,1)}, u32[]{:S(2)}, u32[]{:S(2)}) collective-permute-start(bf16[16,96,512]{2,1,0:T(8,128)(2,1)} %get-tuple-element.321), channel_id=1, source_target_pairs={{0,8},{1,9},{2,10},{3,11},{4,12},{5,13},{6,14},{7,15},{8,0},{9,1},... | collective-permute-start | bytes 4718600 | tf_op jit(solution)/shard_map/ppermute | solution.py:160
  83.6 28.7 %collective-permute-start.14 = (bf16[16,128,512]{1,2,0:T(8,128)(2,1)}, bf16[16,128,512]{1,2,0:T(8,128)(2,1)}, u32[]{:S(2)}, u32[]{:S(2)}) collective-permute-start(bf16[16,128,512]{1,2,0:T(8,128)(2,1)} %get-tuple-element.315), channel_id=1, source_target_pairs={{0,8},{1,9},{2,10},{3,11},{4,12},{5,13},{6,14},{7,15},{8,0},{9,1},... | collective-permute-start | bytes 6291464 | tf_op jit(solution)/shard_map/ppermute | solution.py:160
  96.9 43.1 %collective-permute-start.4 = (bf16[2080,512]{1,0:T(8,128)(2,1)}, bf16[2080,512]{1,0:T(8,128)(2,1)}, u32[]{:S(2)}, u32[]{:S(2)}) collective-permute-start(bf16[2080,512]{1,0:T(8,128)(2,1)} %pad_maximum_fusion.3), channel_id=1, source_target_pairs={{0,8},{1,9},{2,10},{3,11},{4,12},{5,13},{6,14},{7,15},{8,0},{9,1},... | collective-permute-start | bytes 6389768 | tf_op jit(solution)/shard_map/ppermute | solution.py:160
  328.4 144.8 %collective-permute-start.35 = (f32[8,128]{1,0:T(8,128)S(1)}, f32[8,128]{1,0:T(8,128)S(1)}, u32[]{:S(2)}, u32[]{:S(2)}) collective-permute-start(f32[8,128]{1,0:T(8,128)S(1)} %mul.1405), channel_id=1, source_target_pairs={{0,8},{1,9},{2,10},{3,11},{4,12},{5,13},{6,14},{7,15},{8,0},{9,1},... | collective-permute-start | bytes 12296 | tf_op jit(solution)/shard_map/ppermute | solution.py:160
  394.6 90.4 %collective-permute-start.25 = (bf16[16,96,512]{2,1,0:T(8,128)(2,1)}, bf16[16,96,512]{2,1,0:T(8,128)(2,1)}, u32[]{:S(2)}, u32[]{:S(2)}) collective-permute-start(bf16[16,96,512]{2,1,0:T(8,128)(2,1)} %slice.707), channel_id=1, source_target_pairs={{0,8},{1,9},{2,10},{3,11},{4,12},{5,13},{6,14},{7,15},{8,0},{9,1},... | collective-permute-start | bytes 4718600 | tf_op jit(solution)/shard_map/ppermute | solution.py:160
  405.6 127.2 %collective-permute-start.15 = (bf16[16,128,512]{2,1,0:T(8,128)(2,1)}, bf16[16,128,512]{2,1,0:T(8,128)(2,1)}, u32[]{:S(2)}, u32[]{:S(2)}) collective-permute-start(bf16[16,128,512]{2,1,0:T(8,128)(2,1)} %slice.669), channel_id=1, source_target_pairs={{0,8},{1,9},{2,10},{3,11},{4,12},{5,13},{6,14},{7,15},{8,0},{9,1},... | collective-permute-start | bytes 6291464 | tf_op jit(solution)/shard_map/ppermute | solution.py:160
  405.6 133.8 %collective-permute-start.20 = (bf16[16,128,512]{2,1,0:T(8,128)(2,1)}, bf16[16,128,512]{2,1,0:T(8,128)(2,1)}, u32[]{:S(2)}, u32[]{:S(2)}) collective-permute-start(bf16[16,128,512]{2,1,0:T(8,128)(2,1)} %slice.687), channel_id=1, source_target_pairs={{0,8},{1,9},{2,10},{3,11},{4,12},{5,13},{6,14},{7,15},{8,0},{9,1},... | collective-permute-start | bytes 6291464 | tf_op jit(solution)/shard_map/ppermute | solution.py:160
  477.7 7.2 %collective-permute-start.37 = (f32[8,128]{1,0:T(8,128)S(1)}, f32[8,128]{1,0:T(8,128)S(1)}, u32[]{:S(2)}, u32[]{:S(2)}) collective-permute-start(f32[8,128]{1,0:T(8,128)S(1)} %fusion.189), channel_id=1, source_target_pairs={{0,1},{1,0},{2,3},{3,2},{4,5},{5,4},{6,7},{7,6},{8,24},{9,25},{10,... | collective-permute-start | bytes 12296 | tf_op jit(solution)/shard_map/ppermute | solution.py:160
  487.8 31.9 %collective-permute-start.26 = (bf16[8,96,512]{2,1,0:T(8,128)(2,1)}, bf16[8,96,512]{2,1,0:T(8,128)(2,1)}, u32[]{:S(2)}, u32[]{:S(2)}) collective-permute-start(bf16[8,96,512]{2,1,0:T(8,128)(2,1)} %get-tuple-element.278), channel_id=1, source_target_pairs={{0,16},{1,17},{2,18},{3,19},{4,20},{5,21},{6,22},{7,23},{8,9},{9,8... | collective-permute-start | bytes 2359304 | tf_op jit(solution)/shard_map/ppermute | solution.py:160
  488.3 13.6 %collective-permute-start.31 = (f32[32,512]{0,1:T(8,128)S(1)}, f32[32,512]{0,1:T(8,128)S(1)}, u32[]{:S(2)}, u32[]{:S(2)}) collective-permute-start(f32[32,512]{0,1:T(8,128)S(1)} %pad_add_fusion.7), channel_id=1, source_target_pairs={{0,16},{1,17},{2,18},{3,19},{4,20},{5,21},{6,22},{7,23},{8,9},{9,8... | collective-permute-start | bytes 196616 | tf_op jit(solution)/shard_map/ppermute | solution.py:160
  489.4 19.1 %collective-permute-start.39 = (f32[8,128]{1,0:T(8,128)S(1)}, f32[8,128]{1,0:T(8,128)S(1)}, u32[]{:S(2)}, u32[]{:S(2)}) collective-permute-start(f32[8,128]{1,0:T(8,128)S(1)} %add.716), channel_id=1, source_target_pairs={{0,4},{1,5},{2,6},{3,7},{4,0},{5,1},{6,2},{7,3},{8,12},{9,13},{10,... | collective-permute-start | bytes 12296 | tf_op jit(solution)/shard_map/ppermute | solution.py:160
  502.0 7.8 %collective-permute-start.32 = (f32[32,512]{0,1:T(8,128)S(1)}, f32[32,512]{0,1:T(8,128)S(1)}, u32[]{:S(2)}, u32[]{:S(2)}) collective-permute-start(f32[32,512]{0,1:T(8,128)S(1)} %add.700), channel_id=1, source_target_pairs={{0,1},{1,0},{2,3},{3,2},{4,5},{5,4},{6,7},{7,6},{8,24},{9,25},{10,... | collective-permute-start | bytes 196616 | tf_op jit(solution)/shard_map/ppermute | solution.py:160
  509.9 7.5 %collective-permute-start.33 = (f32[32,512]{0,1:T(8,128)S(1)}, f32[32,512]{0,1:T(8,128)S(1)}, u32[]{:S(2)}, u32[]{:S(2)}) collective-permute-start(f32[32,512]{0,1:T(8,128)S(1)} %add.701), channel_id=1, source_target_pairs={{0,2},{1,3},{2,0},{3,1},{4,6},{5,7},{6,4},{7,5},{8,10},{9,11},{10,... | collective-permute-start | bytes 196616 | tf_op jit(solution)/shard_map/ppermute | solution.py:160
  517.4 14.0 %collective-permute-start.34 = (f32[32,512]{0,1:T(8,128)S(1)}, f32[32,512]{0,1:T(8,128)S(1)}, u32[]{:S(2)}, u32[]{:S(2)}) collective-permute-start(f32[32,512]{0,1:T(8,128)S(1)} %add.702), channel_id=1, source_target_pairs={{0,4},{1,5},{2,6},{3,7},{4,0},{5,1},{6,2},{7,3},{8,12},{9,13},{10,... | collective-permute-start | bytes 196616 | tf_op jit(solution)/shard_map/ppermute | solution.py:160
  521.0 11.6 %collective-permute-start.27 = (bf16[4,96,512]{2,1,0:T(8,128)(2,1)S(1)}, bf16[4,96,512]{2,1,0:T(8,128)(2,1)S(1)}, u32[]{:S(2)}, u32[]{:S(2)}) collective-permute-start(bf16[4,96,512]{2,1,0:T(8,128)(2,1)S(1)} %get-tuple-element.293), channel_id=1, source_target_pairs={{0,1},{1,0},{2,3},{3,2},{4,5},{5,4},{6,7},{7,6},{8,24},{9,25},{10,... | collective-permute-start | bytes 1179656 | tf_op jit(solution)/shard_map/ppermute | solution.py:160
  536.2 14.2 %collective-permute-start.16 = (bf16[8,128,512]{2,1,0:T(8,128)(2,1)}, bf16[8,128,512]{2,1,0:T(8,128)(2,1)S(1)}, u32[]{:S(2)}, u32[]{:S(2)}) collective-permute-start(bf16[8,128,512]{2,1,0:T(8,128)(2,1)} %get-tuple-element.276), channel_id=1, source_target_pairs={{0,16},{1,17},{2,18},{3,19},{4,20},{5,21},{6,22},{7,23},{8,9},{9,8... | collective-permute-start | bytes 3145736 | tf_op jit(solution)/shard_map/ppermute | solution.py:160
  542.6 24.4 %collective-permute-start.21 = (bf16[8,128,512]{2,1,0:T(8,128)(2,1)}, bf16[8,128,512]{2,1,0:T(8,128)(2,1)}, u32[]{:S(2)}, u32[]{:S(2)}) collective-permute-start(bf16[8,128,512]{2,1,0:T(8,128)(2,1)} %get-tuple-element.274), channel_id=1, source_target_pairs={{0,16},{1,17},{2,18},{3,19},{4,20},{5,21},{6,22},{7,23},{8,9},{9,8... | collective-permute-start | bytes 3145736 | tf_op jit(solution)/shard_map/ppermute | solution.py:160
  550.7 18.9 %collective-permute-start.17 = (bf16[4,128,512]{2,1,0:T(8,128)(2,1)S(1)}, bf16[4,128,512]{2,1,0:T(8,128)(2,1)S(1)}, u32[]{:S(2)}, u32[]{:S(2)}) collective-permute-start(bf16[4,128,512]{2,1,0:T(8,128)(2,1)S(1)} %get-tuple-element.291), channel_id=1, source_target_pairs={{0,1},{1,0},{2,3},{3,2},{4,5},{5,4},{6,7},{7,6},{8,24},{9,25},{10,... | collective-permute-start | bytes 1572872 | tf_op jit(solution)/shard_map/ppermute | solution.py:160
  568.6 8.4 %collective-permute-start.22 = (bf16[4,128,512]{2,1,0:T(8,128)(2,1)S(1)}, bf16[4,128,512]{2,1,0:T(8,128)(2,1)S(1)}, u32[]{:S(2)}, u32[]{:S(2)}) collective-permute-start(bf16[4,128,512]{2,1,0:T(8,128)(2,1)S(1)} %get-tuple-element.289), channel_id=1, source_target_pairs={{0,1},{1,0},{2,3},{3,2},{4,5},{5,4},{6,7},{7,6},{8,24},{9,25},{10,... | collective-permute-start | bytes 1572872 | tf_op jit(solution)/shard_map/ppermute | solution.py:160
  569.8 9.2 %collective-permute-start.18 = (bf16[2,128,512]{2,1,0:T(8,128)(2,1)S(1)}, bf16[2,128,512]{2,1,0:T(8,128)(2,1)S(1)}, u32[]{:S(2)}, u32[]{:S(2)}) collective-permute-start(bf16[2,128,512]{2,1,0:T(8,128)(2,1)S(1)} %get-tuple-element.299), channel_id=1, source_target_pairs={{0,2},{1,3},{2,0},{3,1},{4,6},{5,7},{6,4},{7,5},{8,10},{9,11},{10,... | collective-permute-start | bytes 786440 | tf_op jit(solution)/shard_map/ppermute | solution.py:160
  (119 other events, 899.5 us)
